TPU v7x, 32 devices: a whole 2x2x4 slice. The times are simulated.
32 devices in a mesh: py: 8 (over z, x), pz: 4 (over y, core).
Axes of the slice: x: 2, y: 2, z: 4, core: 2. Of those that a mesh axis runs over, the one named last changes fastest.
Arguments:
- velocity: float32 [3, 288, 160, 2048], P(None, 'pz', 'py'), may hold values from -40 to 40
Outputs:
- filtered_velocity: float32 [3, 32, 16, 256], P(None, None, 'pz', 'py')
- stresses: float32 [6, 32, 16, 256], P(None, None, 'pz', 'py')
All inputs are finite; a program needn't handle non-finite values.
Results may differ from a plain program's by a relative error of at most 0.00007.
Values sent between devices are 32-bit elements; how exact they have to be, the bound alone decides.
A program may use at most 192 MiB of HBM per device.

v0:
```python
import functools
import numpy as np
import ml_dtypes
import jax
import jax.numpy as jnp
from jax import lax
from jax.sharding import PartitionSpec as P
from jax.experimental import pallas as pl
from jax.experimental.pallas import tpu as pltpu

stress_pairs = ((0, 0), (0, 1), (0, 2), (1, 1), (1, 2), (2, 2))
f32, bf16 = jnp.float32, jnp.bfloat16


def tap(t):
    r = np.arange(-16, 17).astype(np.float64)
    s = np.sum(np.exp(-r * r / 128.0))
    t = np.asarray(t, np.float64)
    return np.where(np.abs(t) <= 16, np.exp(-t * t / 128.0) / s, 0.0)


class Plan:
    def __init__(self, shape, npy, npz):
        _, self.zl, self.yl, self.nx = shape
        self.npy, self.npz = npy, npz
        zl, yl = self.zl, self.yl
        self.oz = (zl * npz - 32) // 8
        self.oy = (yl * npy - 32) // 8
        self.ox = self.nx // 8
        self.kb = self.ox // npy
        self.jq = self.oy // npz
        self.pk = 128 // self.kb
        self.cz = 8 if zl % 8 == 0 else zl
        self.nch = zl // self.cz
        self.zp = -(-self.cz // 8) * 8
        self.kk = yl * self.zp
        cz, nch = self.cz, self.nch
        base = lambda s: (s + 7) // 8 - 4
        self.base_p = [base(zl * p) for p in range(npz)]
        starts = np.array([[zl * p + cz * c for c in range(nch)] for p in range(npz)])
        bases = base(starts)
        self.nic = int(np.max((starts + cz - 1) // 8 - bases + 1))
        self.offs = bases - bases[:, :1]
        self.ni = int(self.offs.max()) + self.nic
        self.groups = -(-self.ni // self.pk)
        z = starts[:, :, None, None] + np.arange(cz)[None, None, None, :]
        i = bases[:, :, None, None] + np.arange(8)[None, None, :, None]
        az = np.where((i >= 0) & (i < self.oz), tap(z - 16 - 8 * i), 0.0)
        az[:, :, self.nic:] = 0.0
        az = np.pad(az, ((0, 0), (0, 0), (0, 0), (0, self.zp - cz)))
        self.az = np.tile(az, (1, 1, 1, yl)).astype(np.float32)
        ay = np.zeros((npy, 8, yl))
        self.mask = np.zeros((npy, self.oy // 8, 8), np.float32)
        for d in range(npy):
            y = yl * d + np.arange(yl)
            for j in range(self.oy):
                w = tap(y - 16 - 8 * j)
                if np.any(w != 0):
                    ay[d, j % 8] += w
                    self.mask[d, j // 8, j % 8] = 1.0
        assert self.mask.sum(axis=1).max() == 1
        self.ay = np.repeat(ay, self.zp, axis=2).astype(np.float32)
        n = np.arange(self.nx)[:, None]
        k = np.arange(self.ox)[None, :]
        t = (n - 8 * k + self.nx // 2) % self.nx - self.nx // 2
        wx = tap(t).astype(np.float32)
        self.wx_hi = wx.astype(ml_dtypes.bfloat16)
        self.wx_lo = (wx - self.wx_hi.astype(np.float32)).astype(ml_dtypes.bfloat16)


def split(val):
    hi = val.astype(bf16)
    return hi, (val - hi.astype(f32)).astype(bf16)


def dot(a, b):
    return jnp.dot(a, b, preferred_element_type=f32)


def sum_block(pn, c, p, d, v_ref, az_ref, ay_ref, acc):
    xt = 512
    wz = az_ref[p, c][: pn.nic]
    wy = ay_ref[d]
    w = (wz[:, None, :] * wy[None, :, :]).reshape(pn.nic * 8, pn.kk)
    w_hi = w.astype(bf16).astype(f32)
    w2 = jnp.concatenate([w_hi, w - w_hi], axis=0).astype(bf16)
    off = (pn.zl * p + pn.cz * c + 7) // 8 - (pn.zl * p + 7) // 8
    m = pn.nic * 8

    def tile(x, carry):
        xs = pl.ds(pl.multiple_of(x * xt, xt), xt)
        comps = []
        for a in range(3):
            blk = v_ref[a, :, :, xs]
            if pn.zp > pn.cz:
                blk = jnp.concatenate([blk, jnp.zeros((pn.yl, pn.zp - pn.cz, xt), f32)], axis=1)
            comps.append(blk.reshape(pn.kk, xt))
        for f in range(9):
            if f < 3:
                val = comps[f]
            else:
                a, b = stress_pairs[f - 3]
                val = comps[a] * comps[b]
            hi, lo = split(val)
            r = dot(w2, hi) + dot(w2, lo)
            r = (r[:m] + r[m:]).reshape(pn.nic, 8, xt)
            acc[f, pl.ds(off, pn.nic), :, xs] += r
        return carry

    lax.fori_loop(0, pn.nx // xt, tile, 0)


def first_group(pn, g, acc, wh_ref, wl_ref, out_ref):
    rows = min(pn.pk, pn.ni - g * pn.pk)
    parts = []
    for q in range(rows):
        a = acc[:, g * pn.pk + q].reshape(72, pn.nx)
        hi, lo = split(a)
        parts.append(dot(hi, wh_ref[...]) + (dot(lo, wh_ref[...]) + dot(hi, wl_ref[...])))
    lane = lax.broadcasted_iota(jnp.int32, (72, 128), 1)
    for m in range(pn.npy):
        mg, mo = divmod(m * pn.kb, 128)
        res = jnp.zeros((72, 128), f32)
        for q in range(rows):
            piece = parts[q][:, mg * 128:(mg + 1) * 128]
            shift = (q * pn.kb - mo) % 128
            if shift:
                piece = pltpu.roll(piece, shift, 1)
            res = jnp.where((lane >= q * pn.kb) & (lane < (q + 1) * pn.kb), piece, res)
        out_ref[m, g] = res.reshape(9, 8, 128)


def local_kernel(pn, v_ref, az_ref, ay_ref, wh_ref, wl_ref, out_ref, acc):
    c = pl.program_id(0)
    d, p = lax.axis_index("py"), lax.axis_index("pz")

    @pl.when(c == 0)
    def _():
        acc[...] = jnp.zeros_like(acc)

    sum_block(pn, c, p, d, v_ref, az_ref, ay_ref, acc)

    @pl.when(c == pn.nch - 1)
    def _():
        for g in range(pn.groups):
            first_group(pn, g, acc, wh_ref, wl_ref, out_ref)


def local_sums(pn, velocity):
    whole = lambda a: pl.BlockSpec(a.shape, lambda c: (0,) * a.ndim)
    tables = [pn.az, pn.ay, pn.wx_hi, pn.wx_lo]
    return pl.pallas_call(
        functools.partial(local_kernel, pn),
        grid=(pn.nch,),
        in_specs=[pl.BlockSpec((3, pn.yl, pn.cz, pn.nx), lambda c: (0, 0, c, 0))] + [whole(t) for t in tables],
        out_specs=pl.BlockSpec((pn.npy, pn.groups, 9, 8, 128), lambda c: (0, 0, 0, 0, 0)),
        out_shape=jax.ShapeDtypeStruct((pn.npy, pn.groups, 9, 8, 128), f32),
        scratch_shapes=[pltpu.VMEM((9, pn.ni, 8, pn.nx), f32)],
        compiler_params=pltpu.CompilerParams(vmem_limit_bytes=50 * 2**20),
    )(velocity, *[jnp.asarray(t) for t in tables])


def exchange_kernel(pn, in_ref, vel_ref, str_ref, rec_y, snd_z, rec_z, sy, ry, sz, rz):
    d, p = lax.axis_index("py"), lax.axis_index("pz")
    npy, npz, jq, kb = pn.npy, pn.npz, pn.jq, pn.kb
    mesh_id = pl.DeviceIdType.MESH
    barrier = pltpu.get_barrier_semaphore()
    for o in range(1, npy):
        pl.semaphore_signal(barrier, inc=1, device_id=(lax.rem(d + o, npy), p), device_id_type=mesh_id)
    for o in range(1, npz):
        pl.semaphore_signal(barrier, inc=1, device_id=(d, lax.rem(p + o, npz)), device_id_type=mesh_id)
    pl.semaphore_wait(barrier, npy + npz - 2)

    y_copies = []
    for g in range(pn.groups):
        y_copies.append([])
        for o in range(1, npy):
            to = lax.rem(d + o, npy)
            copy = pltpu.make_async_remote_copy(
                src_ref=in_ref.at[to, g], dst_ref=rec_y.at[d, g], send_sem=sy.at[g, o], recv_sem=ry.at[g, o],
                device_id=(to, p), device_id_type=mesh_id)
            copy.start()
            y_copies[g].append(copy)
    rec_y[d] = in_ref[d]
    z_copies = []

    row = lax.broadcasted_iota(jnp.int32, (9, 8, 128), 1)
    for g in range(pn.groups):
        for copy in y_copies[g]:
            copy.wait()
        for h in range(pn.oy // 8):
            total = jnp.zeros((9, 8, 128), f32)
            for s in range(npy):
                rows = np.nonzero(pn.mask[s, h])[0]
                if len(rows) == 0:
                    continue
                val = rec_y[s, g]
                if len(rows) < 8:
                    val = jnp.where((row >= int(rows[0])) & (row <= int(rows[-1])), val, 0.0)
                total = total + val
            for part in range(8 // jq):
                snd_z[h * (8 // jq) + part, g] = total[:, part * jq:(part + 1) * jq, :]
        for o in range(1, npz):
            to = lax.rem(p + o, npz)
            copy = pltpu.make_async_remote_copy(
                src_ref=snd_z.at[to, g], dst_ref=rec_z.at[p, g], send_sem=sz.at[g, o], recv_sem=rz.at[g, o],
                device_id=(d, to), device_id_type=mesh_id)
            copy.start()
            z_copies.append(copy)
    rec_z[p] = snd_z[p]
    for copy in z_copies:
        copy.wait()

    for i in range(pn.oz):
        total = jnp.zeros((9, jq, kb), f32)
        for s in range(npz):
            n = i - pn.base_p[s]
            if 0 <= n < pn.ni:
                g, q = divmod(n, pn.pk)
                total = total + rec_z[s, g, :, :, q * kb:(q + 1) * kb]
        vel_ref[:, i] = total[:3]
        for n, (a, b) in enumerate(stress_pairs):
            str_ref[n, i] = total[3 + n] - total[a] * total[b]


def exchange(pn, packed):
    vmem = pl.BlockSpec(memory_space=pltpu.VMEM)
    zbuf = pltpu.VMEM((pn.npz, pn.groups, 9, pn.jq, 128), f32)
    sems = [pltpu.SemaphoreType.DMA((pn.groups, n)) for n in (pn.npy, pn.npy, pn.npz, pn.npz)]
    return pl.pallas_call(
        functools.partial(exchange_kernel, pn),
        in_specs=[vmem],
        out_specs=(vmem, vmem),
        out_shape=tuple(jax.ShapeDtypeStruct((n, pn.oz, pn.jq, pn.kb), f32) for n in (3, 6)),
        scratch_shapes=[pltpu.VMEM((pn.npy, pn.groups, 9, 8, 128), f32), zbuf, zbuf] + sems,
        compiler_params=pltpu.CompilerParams(
            collective_id=0, has_side_effects=True, vmem_limit_bytes=32 * 2**20
        ),
    )(packed)


def on_device(npy, npz, velocity):
    pn = Plan(velocity.shape, npy, npz)
    packed = local_sums(pn, jnp.transpose(velocity, (0, 2, 1, 3)))
    return exchange(pn, packed)


def solution(mesh):
    return jax.shard_map(
        functools.partial(on_device, mesh.shape["py"], mesh.shape["pz"]),
        mesh=mesh,
        in_specs=(P(None, "pz", "py", None),),
        out_specs=(P(None, None, "pz", "py"), P(None, None, "pz", "py")),
        check_vma=False,
    )
```

profile of v0, /device:TPU:0, one launch (start us, length us, event | category | flops | bytes accessed | tf_op | source)
XLA Modules:
  0.0 75.6 jit_solution(4191337198173041775)
XLA Ops:
  0.6 0.0 copy-start
  0.6 1.2 %copy-done = bf16[2048,256]{1,0:T(8,128)(2,1)S(1)} copy-done((bf16[2048,256]{1,0:T(8,128)(2,1)S(1)}, bf16[2048,256]{1,0:T(8,128)(2,1)}, u32[]{:S(2)}) %copy-start) | copy-done | bytes 1048600
  1.9 0.0 copy-start.1
  1.9 1.2 %copy-done.1 = bf16[2048,256]{1,0:T(8,128)(2,1)S(1)} copy-done((bf16[2048,256]{1,0:T(8,128)(2,1)S(1)}, bf16[2048,256]{1,0:T(8,128)(2,1)}, u32[]{:S(2)}) %copy-start.1) | copy-done | bytes 1048600
  3.1 0.0 copy-start.2
  3.1 1.0 %copy-done.2 = f32[4,9,8,160]{3,2,1,0:T(8,128)S(1)} copy-done((f32[4,9,8,160]{3,2,1,0:T(8,128)S(1)}, f32[4,9,8,160]{3,2,1,0:T(8,128)}, u32[]{:S(2)}) %copy-start.2) | copy-done | bytes 184344
  4.0 0.0 copy-start.3
  4.0 0.8 %copy-done.3 = f32[8,8,160]{2,1,0:T(8,128)S(1)} copy-done((f32[8,8,160]{2,1,0:T(8,128)S(1)}, f32[8,8,160]{2,1,0:T(8,128)}, u32[]{:S(2)}) %copy-start.3) | copy-done | bytes 40984
  4.9 33.7 %shard_map.68.in_ref = f32[8,4,9,8,128]{4,3,2,1,0:T(8,128)S(1)} custom-call(f32[3,20,72,2048]{3,2,1,0:T(8,128)} %bitcast.1, f32[4,9,8,160]{3,2,1,0:T(8,128)S(1)} %copy-done.2, f32[8,8,160]{2,1,0:T(8,128)S(1)} %copy-done.3, bf16[2048,256]{1,0:T(8,128)(2,1)S(1)} %copy-done.1, bf16[2048,256]{1,0:T(8,128)(2,1)S(1)} %copy-done), custom_call_target="tpu_custom_call" | custom-call | tf_op jit(solution)/shard_map/pallas_call | solution.py:152
  38.6 35.6 %shard_map.69 = (f32[3,32,4,32]{3,2,1,0:T(4,128)S(1)}, f32[6,32,4,32]{3,2,1,0:T(4,128)S(1)}) custom-call(f32[8,4,9,8,128]{4,3,2,1,0:T(8,128)S(1)} %shard_map.68.in_ref), custom_call_target="tpu_custom_call" | custom-call | tf_op jit(solution)/shard_map/pallas_call | solution.py:230
  74.2 0.7 copy.9
  74.9 0.7 copy.10
Async XLA Ops:
  0.6 1.2 %copy-start = (bf16[2048,256]{1,0:T(8,128)(2,1)S(1)}, bf16[2048,256]{1,0:T(8,128)(2,1)}, u32[]{:S(2)}) copy-start(bf16[2048,256]{1,0:T(8,128)(2,1)} %constant.11.clone.wl_ref) | copy-start | bytes 3145732
  1.9 1.2 %copy-start.1 = (bf16[2048,256]{1,0:T(8,128)(2,1)S(1)}, bf16[2048,256]{1,0:T(8,128)(2,1)}, u32[]{:S(2)}) copy-start(bf16[2048,256]{1,0:T(8,128)(2,1)} %constant.10.clone.wh_ref) | copy-start | bytes 3145732
  3.1 1.0 %copy-start.2 = (f32[4,9,8,160]{3,2,1,0:T(8,128)S(1)}, f32[4,9,8,160]{3,2,1,0:T(8,128)}, u32[]{:S(2)}) copy-start(f32[4,9,8,160]{3,2,1,0:T(8,128)} %constant.8.clone.az_ref) | copy-start | bytes 552964
  4.0 0.8 %copy-start.3 = (f32[8,8,160]{2,1,0:T(8,128)S(1)}, f32[8,8,160]{2,1,0:T(8,128)}, u32[]{:S(2)}) copy-start(f32[8,8,160]{2,1,0:T(8,128)} %constant.9.clone.ay_ref) | copy-start | bytes 122884
where the time goes:
time: 75.9 us; the launch traced here: 75.6 us
  Pallas kernels  69.3 us (91%)
  local copies, waits for them, and re-layouts  5.67 us (7%)
    pallas_call x1, Pallas kernels, exchange(): pl.pallas_call(functools.partial(exchange_kernel, pn), in_specs=[vmem], o...  35.6 us
    pallas_call x1, Pallas kernels, local_sums(): pl.pallas_call(functools.partial(local_kernel, pn), grid=(pn.nch,), in_sp...  33.7 us
    unnamed x10, local copies, waits for them, and re-layouts  5.67 us

commit v1 on v0

--- a/solution.py
+++ b/solution.py
@@ -239,10 +239,288 @@
     )(packed)
 
 
+class Fast:
+    def __init__(self, pn):
+        self.npy, self.npz = pn.npy, pn.npz
+        npy, npz = pn.npy, pn.npz
+        self.xt = pn.nx // npy
+        self.kb = pn.kb
+        self.own = pn.oz // npz
+        self.ok = pn.kb == 32 and pn.oz % npz == 0 and self.own % 4 == 0 and pn.oy % 8 == 0 and pn.oy % npz == 0
+        self.ok = self.ok and pn.jq in (4, 8) and npy >= 4 and npz >= 2 and pn.zl % 8 == 0 and pn.mask.sum(axis=1).max() == 1
+        if not self.ok:
+            return
+        self.cz = next(c for c in (24, 16, 8) if pn.zl % c == 0)
+        self.nch = pn.zl // self.cz
+        self.kk = pn.yl * self.cz
+        self.nic = (self.cz - 1) // 8 + 5
+        self.groups = self.own // 4 + 2
+        self.ng = self.own // 4
+        self.slots = self.groups * 4
+        first = [(pn.zl * p) // 8 - 4 - (self.own * p - 4) for p in range(npz)]
+        self.first = first
+        self.step = first[1] - first[0]
+        self.ok = all(f == first[0] + self.step * p for p, f in enumerate(first))
+        self.ok = self.ok and min(first) >= 0 and max(first) + (self.nch - 1) * self.cz // 8 + self.nic <= self.slots
+        if not self.ok:
+            return
+        z0 = np.array([[pn.zl * p + self.cz * c for c in range(self.nch)] for p in range(npz)])
+        z = z0[:, :, None, None] + np.arange(self.cz)
+        i = (z0 // 8 - 4)[:, :, None, None] + np.arange(self.nic)[:, None]
+        az = np.where((i >= 0) & (i < pn.oz), tap(z - 16 - 8 * i), 0.0)
+        az = np.pad(az, ((0, 0), (0, 0), (0, -self.nic % 8), (0, 0)))
+        self.az = np.tile(az, (1, 1, 1, pn.yl)).astype(np.float32)
+        ay = np.zeros((npy, 8, pn.yl))
+        for d in range(npy):
+            for j in range(pn.oy):
+                w = tap(pn.yl * d + np.arange(pn.yl) - 16 - 8 * j)
+                if np.any(w != 0):
+                    ay[d, j % 8] += w
+        self.ay = np.repeat(ay, self.cz, axis=2).astype(np.float32)
+        n = np.arange(self.xt)[:, None]
+        k = np.arange(32)[None, :]
+        main = tap(n - 8 * k)
+        edge = np.where(k >= 16, tap(n - 8 * k + self.xt), tap(n - 8 * k - self.xt))
+        wx = np.concatenate([main, edge], axis=1).astype(np.float32)
+        hi = wx.astype(ml_dtypes.bfloat16)
+        lo = (wx - hi.astype(np.float32)).astype(ml_dtypes.bfloat16)
+        t = np.zeros((2, self.xt, 256), ml_dtypes.bfloat16)
+        for h in range(2):
+            t[0, :, 128 * h:128 * h + 32] = hi[:, 32 * h:32 * h + 32]
+            t[0, :, 128 * h + 32:128 * h + 64] = lo[:, 32 * h:32 * h + 32]
+            t[1, :, 128 * h:128 * h + 32] = hi[:, 32 * h:32 * h + 32]
+        self.wx = t.reshape(2 * self.xt, 256)
+
+
+def fused_kernel(pn, fs, v_hbm, az_hbm, ay_hbm, wx_hbm, vel_ref, str_ref,
+                 vbuf, az, ay, wx, w2, acc, part, rec_h, rec_y, snd_z, rec_z,
+                 sv, st, sh, rh, sy, ry, sz, rz):
+    d, p = lax.axis_index("py"), lax.axis_index("pz")
+    npy, npz, jq, kb = pn.npy, pn.npz, pn.jq, pn.kb
+    xt, cz, nch, nic, groups, ng = fs.xt, fs.cz, fs.nch, fs.nic, fs.groups, fs.ng
+    mesh_id = pl.DeviceIdType.MESH
+
+    def load(s, c):
+        x = pl.multiple_of(lax.rem(d + s, npy) * xt, xt)
+        b = lax.rem(s, 2)
+        return pltpu.make_async_copy(
+            v_hbm.at[:, :, pl.ds(c * cz, cz), pl.ds(x, xt)],
+            vbuf.at[b, :, :, pl.ds(c * cz, cz), :], sv.at[b, c])
+
+    tables = [pltpu.make_async_copy(az_hbm.at[p], az, st.at[0]),
+              pltpu.make_async_copy(ay_hbm.at[d], ay, st.at[1]),
+              pltpu.make_async_copy(wx_hbm, wx, st.at[2])]
+    for t in tables:
+        t.start()
+    for c in range(nch):
+        load(0, c).start()
+
+    barrier = pltpu.get_barrier_semaphore()
+    for o in range(1, npy):
+        pl.semaphore_signal(barrier, inc=1, device_id=(lax.rem(d + o, npy), p), device_id_type=mesh_id)
+    for o in range(1, npz):
+        pl.semaphore_signal(barrier, inc=1, device_id=(d, lax.rem(p + o, npz)), device_id_type=mesh_id)
+
+    part[...] = jnp.zeros_like(part)
+    for t in tables:
+        t.wait()
+    for c in range(nch):
+        wz = az[c][:nic]
+        w = (wz[:, None, :] * ay[...][None, :, :]).reshape(nic * 8, fs.kk)
+        w_hi = w.astype(bf16)
+        w2[c, :nic * 8] = w_hi.astype(f32)
+        w2[c, nic * 8:] = w - w_hi.astype(f32)
+    pl.semaphore_wait(barrier, npy + npz - 2)
+
+    lane = lax.broadcasted_iota(jnp.int32, (8, 128), 1)
+    sub = lax.rem(lane, 32)
+    m = nic * 8
+
+    def up(b):
+        return pltpu.make_async_remote_copy(
+            src_ref=part.at[b, groups - 1], dst_ref=rec_h.at[b, 0], send_sem=sh.at[b, 0], recv_sem=rh.at[b, 0],
+            device_id=(d, lax.rem(p + 1, npz)), device_id_type=mesh_id)
+
+    def down(b):
+        return pltpu.make_async_remote_copy(
+            src_ref=part.at[b, 0], dst_ref=rec_h.at[b, 1], send_sem=sh.at[b, 1], recv_sem=rh.at[b, 1],
+            device_id=(d, lax.rem(p + npz - 1, npz)), device_id_type=mesh_id)
+
+    def across(b):
+        return pltpu.make_async_remote_copy(
+            src_ref=part.at[b, pl.ds(1, ng)], dst_ref=rec_y.at[d], send_sem=sy.at[b], recv_sem=ry.at[b],
+            device_id=(lax.rem(d + b, npy), p), device_id_type=mesh_id)
+
+    def halo_start(b):
+        @pl.when(p < npz - 1)
+        def _():
+            up(b).start()
+
+        @pl.when(p > 0)
+        def _():
+            down(b).start()
+
+    def halo_finish(b):
+        @pl.when(p > 0)
+        def _():
+            up(b).wait_recv()
+            part[b, 1] += rec_h[b, 0]
+
+        @pl.when(p < npz - 1)
+        def _():
+            down(b).wait_recv()
+            part[b, ng] += rec_h[b, 1]
+
+    def halo_sent(b):
+        @pl.when(p < npz - 1)
+        def _():
+            up(b).wait_send()
+
+        @pl.when(p > 0)
+        def _():
+            down(b).wait_send()
+
+    def block(s, carry):
+        b = lax.rem(s, 2)
+
+        @pl.when(s < npy - 1)
+        def _():
+            for c in range(nch):
+                load(s + 1, c).start()
+
+        acc[...] = jnp.zeros_like(acc)
+        for c in range(nch):
+            load(s, c).wait()
+            wt = w2[c].astype(bf16)
+            row = fs.first[0] + fs.step * p + c * (cz // 8)
+            for f in range(9):
+                if f < 3:
+                    val = vbuf[b, f, :, c * cz:(c + 1) * cz, :]
+                else:
+                    a1, a2 = stress_pairs[f - 3]
+                    val = vbuf[b, a1, :, c * cz:(c + 1) * cz, :] * vbuf[b, a2, :, c * cz:(c + 1) * cz, :]
+                hi, lo = split(val.reshape(fs.kk, xt))
+                r = dot(wt, hi)
+                r = r[:m] + r[m:] + dot(wt[:m], lo)
+                acc[f, pl.ds(row, nic)] += r.reshape(nic, 8, xt)
+
+        left, right = lax.rem(s + npy - 1, npy), lax.rem(s + 1, npy)
+        for f3 in range(3):
+            hi, lo = split(acc[3 * f3:3 * f3 + 3].reshape(3 * fs.slots * 8, xt))
+            r = dot(jnp.concatenate([hi, lo], axis=1), wx[...])
+            r = r.reshape(3, fs.slots, 8, 256)
+            for f in range(3):
+                for g in range(groups):
+                    pair = []
+                    for h in range(2):
+                        res = jnp.zeros((8, 128), f32)
+                        for q in range(4):
+                            piece = r[f, 4 * g + q, :, 128 * h:128 * h + 128]
+                            piece = piece + pltpu.roll(piece, 96, 1)
+                            if q:
+                                piece = pltpu.roll(piece, 32 * q, 1)
+                            res = jnp.where((lane >= 32 * q) & (lane < 32 * q + 32), piece, res)
+                        pair.append(res)
+                    part[s, g, 3 * f3 + f] += pair[0]
+                    part[left, g, 3 * f3 + f] += jnp.where(sub >= 16, pair[1], 0.0)
+                    part[right, g, 3 * f3 + f] += jnp.where(sub < 16, pair[1], 0.0)
+
+        @pl.when(s >= 3)
+        def _():
+            halo_finish(s - 2)
+            across(s - 2).start()
+
+        @pl.when(s >= 2)
+        def _():
+            halo_start(s - 1)
+        return carry
+
+    lax.fori_loop(0, npy, block, 0)
+    halo_start(npy - 1)
+    halo_start(0)
+    for o in (npy - 2, npy - 1):
+        halo_finish(o)
+        across(o).start()
+    halo_finish(0)
+    rec_y[d] = part[0, 1:1 + ng]
+    for o in range(1, npy):
+        across(o).wait()
+    for o in range(npy):
+        halo_sent(o)
+
+    rowi = lax.broadcasted_iota(jnp.int32, (ng, 9, 8, 128), 2)
+    for h in range(pn.oy // 8):
+        total = jnp.zeros((ng, 9, 8, 128), f32)
+        for s in range(npy):
+            rows = np.nonzero(pn.mask[s, h])[0]
+            if len(rows) == 0:
+                continue
+            val = rec_y[s]
+            if len(rows) < 8:
+                val = jnp.where((rowi >= int(rows[0])) & (rowi <= int(rows[-1])), val, 0.0)
+            total = total + val
+        for q in range(8 // jq):
+            snd_z[h * (8 // jq) + q] = total[:, :, q * jq:(q + 1) * jq, :]
+    copies = []
+    for o in range(1, npz):
+        to = lax.rem(p + o, npz)
+        copy = pltpu.make_async_remote_copy(
+            src_ref=snd_z.at[to], dst_ref=rec_z.at[p], send_sem=sz.at[o], recv_sem=rz.at[o],
+            device_id=(d, to), device_id_type=mesh_id)
+        copy.start()
+        copies.append(copy)
+    rec_z[p] = snd_z[p]
+    for copy in copies:
+        copy.wait()
+    for s in range(npz):
+        for g in range(ng):
+            t = rec_z[s, g]
+            tau = [t[3 + n] - t[a] * t[b] for n, (a, b) in enumerate(stress_pairs)]
+            for q in range(4):
+                i = fs.own * s + 4 * g + q
+                for n in range(3):
+                    vel_ref[n, i] = t[n, :, q * kb:(q + 1) * kb]
+                for n in range(6):
+                    str_ref[n, i] = tau[n][:, q * kb:(q + 1) * kb]
+
+
+def fused(pn, fs, velocity):
+    vmem = pl.BlockSpec(memory_space=pltpu.VMEM)
+    hbm = pl.BlockSpec(memory_space=pl.ANY)
+    npy, npz, ng = pn.npy, pn.npz, fs.ng
+    dma = lambda *n: pltpu.SemaphoreType.DMA(n)
+    return pl.pallas_call(
+        functools.partial(fused_kernel, pn, fs),
+        in_specs=[hbm] * 4,
+        out_specs=(vmem, vmem),
+        out_shape=tuple(jax.ShapeDtypeStruct((n, pn.oz, pn.jq, pn.kb), f32) for n in (3, 6)),
+        scratch_shapes=[
+            pltpu.VMEM((2, 3, pn.yl, pn.zl, fs.xt), f32),
+            pltpu.VMEM(fs.az.shape[1:], f32),
+            pltpu.VMEM(fs.ay.shape[1:], f32),
+            pltpu.VMEM(fs.wx.shape, bf16),
+            pltpu.VMEM((fs.nch, 2 * fs.nic * 8, fs.kk), f32),
+            pltpu.VMEM((9, fs.slots, 8, fs.xt), f32),
+            pltpu.VMEM((npy, fs.groups, 9, 8, 128), f32),
+            pltpu.VMEM((npy, 2, 9, 8, 128), f32),
+            pltpu.VMEM((npy, ng, 9, 8, 128), f32),
+            pltpu.VMEM((npz, ng, 9, pn.jq, 128), f32),
+            pltpu.VMEM((npz, ng, 9, pn.jq, 128), f32),
+            dma(2, fs.nch), dma(3), dma(npy, 2), dma(npy, 2), dma(npy), dma(npy), dma(npz), dma(npz),
+        ],
+        compiler_params=pltpu.CompilerParams(
+            collective_id=0, has_side_effects=True, vmem_limit_bytes=50 * 2**20
+        ),
+    )(velocity, *[jnp.asarray(t) for t in (fs.az, fs.ay, fs.wx)])
+
+
 def on_device(npy, npz, velocity):
     pn = Plan(velocity.shape, npy, npz)
-    packed = local_sums(pn, jnp.transpose(velocity, (0, 2, 1, 3)))
-    return exchange(pn, packed)
+    fs = Fast(pn)
+    v = jnp.transpose(velocity, (0, 2, 1, 3))
+    if fs.ok:
+        return fused(pn, fs, v)
+    return exchange(pn, local_sums(pn, v))
 
 
 def solution(mesh):

time: 75.9 us -> 54.5 us (0.72)
  Pallas kernels: 69.3 us -> 49.3 us
  local copies, waits for them, and re-layouts: 5.67 us -> 4.2 us
    pallas_call x2 -> x1, Pallas kernels: 69.3 us -> 49.3 us  [fused(): pl.pallas_call(functools.partial(fused_kernel, pn, fs), in_specs=[hbm] *...]
    unnamed x10 -> x8, local copies, waits for them, and re-layouts: 5.67 us -> 4.2 us
where the time goes in v1:
time: 54.5 us; the launch traced here: 54.2 us
  Pallas kernels  49.3 us (90%)
  local copies, waits for them, and re-layouts  4.2 us (8%)
  between operations  0.65 us (1%)
    pallas_call x1, Pallas kernels, fused(): pl.pallas_call(functools.partial(fused_kernel, pn, fs), in_specs=[hbm] *...  49.3 us
    unnamed x8, local copies, waits for them, and re-layouts  4.2 us

profile of v1, /device:TPU:0, one launch (start us, length us, event | category | flops | bytes accessed | tf_op | source)
XLA Modules:
  0.0 54.2 jit_solution(5967404859137186654)
XLA Ops:
  0.6 0.0 copy-start
  0.6 0.9 %copy-done = bf16[512,256]{1,0:T(8,128)(2,1)S(1)} copy-done((bf16[512,256]{1,0:T(8,128)(2,1)S(1)}, bf16[512,256]{1,0:T(8,128)(2,1)}, u32[]{:S(2)}) %copy-start) | copy-done | bytes 262168
  1.6 0.0 copy-start.1
  1.6 0.9 %copy-done.1 = f32[4,3,8,480]{3,2,1,0:T(8,128)S(1)} copy-done((f32[4,3,8,480]{3,2,1,0:T(8,128)S(1)}, f32[4,3,8,480]{3,2,1,0:T(8,128)}, u32[]{:S(2)}) %copy-start.1) | copy-done | bytes 184344
  2.5 0.0 copy-start.2
  2.5 0.9 %copy-done.2 = f32[8,8,480]{2,1,0:T(8,128)S(1)} copy-done((f32[8,8,480]{2,1,0:T(8,128)S(1)}, f32[8,8,480]{2,1,0:T(8,128)}, u32[]{:S(2)}) %copy-start.2) | copy-done | bytes 122904
  3.4 49.3 %shard_map.59 = (f32[3,32,4,32]{3,2,1,0:T(4,128)S(1)}, f32[6,32,4,32]{3,2,1,0:T(4,128)S(1)}) custom-call(f32[3,20,72,2048]{3,2,1,0:T(8,128)} %bitcast.1, f32[4,3,8,480]{3,2,1,0:T(8,128)S(1)} %copy-done.1, f32[8,8,480]{2,1,0:T(8,128)S(1)} %copy-done.2, bf16[512,256]{1,0:T(8,128)(2,1)S(1)} %copy-done), custom_call_target="tpu_custom_call" | custom-call | tf_op jit(solution)/shard_map/pallas_call | solution.py:492
  52.8 0.7 %copy.8 = f32[3,32,4,32]{3,2,1,0:T(4,128)} copy(f32[3,32,4,32]{3,2,1,0:T(4,128)S(1)} %get-tuple-element.4) | data formatting | bytes 98304
  53.4 0.7 %copy.9 = f32[6,32,4,32]{3,2,1,0:T(4,128)} copy(f32[6,32,4,32]{3,2,1,0:T(4,128)S(1)} %get-tuple-element.5) | data formatting | bytes 196608
Async XLA Ops:
  0.6 1.0 %copy-start = (bf16[512,256]{1,0:T(8,128)(2,1)S(1)}, bf16[512,256]{1,0:T(8,128)(2,1)}, u32[]{:S(2)}) copy-start(bf16[512,256]{1,0:T(8,128)(2,1)} %constant.8.clone.wx_hbm) | copy-start | bytes 786436
  1.6 0.9 %copy-start.1 = (f32[4,3,8,480]{3,2,1,0:T(8,128)S(1)}, f32[4,3,8,480]{3,2,1,0:T(8,128)}, u32[]{:S(2)}) copy-start(f32[4,3,8,480]{3,2,1,0:T(8,128)} %constant.6.clone.az_hbm) | copy-start | bytes 552964
  2.5 0.9 %copy-start.2 = (f32[8,8,480]{2,1,0:T(8,128)S(1)}, f32[8,8,480]{2,1,0:T(8,128)}, u32[]{:S(2)}) copy-start(f32[8,8,480]{2,1,0:T(8,128)} %constant.7.clone.ay_hbm) | copy-start | bytes 368644

commit v2 on v1

--- a/solution.py
+++ b/solution.py
@@ -284,12 +284,11 @@
         wx = np.concatenate([main, edge], axis=1).astype(np.float32)
         hi = wx.astype(ml_dtypes.bfloat16)
         lo = (wx - hi.astype(np.float32)).astype(ml_dtypes.bfloat16)
-        t = np.zeros((2, self.xt, 256), ml_dtypes.bfloat16)
-        for h in range(2):
-            t[0, :, 128 * h:128 * h + 32] = hi[:, 32 * h:32 * h + 32]
-            t[0, :, 128 * h + 32:128 * h + 64] = lo[:, 32 * h:32 * h + 32]
-            t[1, :, 128 * h:128 * h + 32] = hi[:, 32 * h:32 * h + 32]
-        self.wx = t.reshape(2 * self.xt, 256)
+        t = np.zeros((4, 3, self.xt, 2, 4, 32), ml_dtypes.bfloat16)
+        for q in range(4):
+            for n, val in enumerate((hi, hi, lo)):
+                t[q, n, :, :, q] = val.reshape(self.xt, 2, 32)
+        self.wx = t.reshape(12 * self.xt, 256)
 
 
 def fused_kernel(pn, fs, v_hbm, az_hbm, ay_hbm, wx_hbm, vel_ref, str_ref,
@@ -332,8 +331,7 @@
         w2[c, nic * 8:] = w - w_hi.astype(f32)
     pl.semaphore_wait(barrier, npy + npz - 2)
 
-    lane = lax.broadcasted_iota(jnp.int32, (8, 128), 1)
-    sub = lax.rem(lane, 32)
+    sub = lax.rem(lax.broadcasted_iota(jnp.int32, (groups, 9, 8, 128), 3), 32)
     m = nic * 8
 
     def up(b):
@@ -400,30 +398,30 @@
                     a1, a2 = stress_pairs[f - 3]
                     val = vbuf[b, a1, :, c * cz:(c + 1) * cz, :] * vbuf[b, a2, :, c * cz:(c + 1) * cz, :]
                 hi, lo = split(val.reshape(fs.kk, xt))
-                r = dot(wt, hi)
-                r = r[:m] + r[m:] + dot(wt[:m], lo)
+                if f % 2 == 0:
+                    r = dot(wt, hi)
+                    r = r[:m] + r[m:] + dot(wt[:m], lo)
+                else:
+                    r_lo = dot(wt[:m], lo)
+                    r = dot(wt, hi)
+                    r = r[:m] + r[m:] + r_lo
                 acc[f, pl.ds(row, nic)] += r.reshape(nic, 8, xt)
 
         left, right = lax.rem(s + npy - 1, npy), lax.rem(s + 1, npy)
-        for f3 in range(3):
-            hi, lo = split(acc[3 * f3:3 * f3 + 3].reshape(3 * fs.slots * 8, xt))
-            r = dot(jnp.concatenate([hi, lo], axis=1), wx[...])
-            r = r.reshape(3, fs.slots, 8, 256)
-            for f in range(3):
-                for g in range(groups):
-                    pair = []
-                    for h in range(2):
-                        res = jnp.zeros((8, 128), f32)
-                        for q in range(4):
-                            piece = r[f, 4 * g + q, :, 128 * h:128 * h + 128]
-                            piece = piece + pltpu.roll(piece, 96, 1)
-                            if q:
-                                piece = pltpu.roll(piece, 32 * q, 1)
-                            res = jnp.where((lane >= 32 * q) & (lane < 32 * q + 32), piece, res)
-                        pair.append(res)
-                    part[s, g, 3 * f3 + f] += pair[0]
-                    part[left, g, 3 * f3 + f] += jnp.where(sub >= 16, pair[1], 0.0)
-                    part[right, g, 3 * f3 + f] += jnp.where(sub < 16, pair[1], 0.0)
+        res = None
+        for h in range(2):
+            cols = []
+            for q in (2 * h, 2 * h + 1):
+                a = jnp.concatenate([acc[f, 4 * g + q] for g in range(groups) for f in range(9)], axis=0)
+                hi, lo = split(a)
+                cols += [hi, lo, hi]
+            r = dot(jnp.concatenate(cols, axis=1), wx[6 * xt * h:6 * xt * (h + 1)])
+            res = r if res is None else res + r
+        main = res[:, :128].reshape(groups, 9, 8, 128)
+        edge = res[:, 128:].reshape(groups, 9, 8, 128)
+        part[s] += main
+        part[left] += jnp.where(sub >= 16, edge, 0.0)
+        part[right] += jnp.where(sub < 16, edge, 0.0)
 
         @pl.when(s >= 3)
         def _():
@@ -486,7 +484,7 @@
 
 def fused(pn, fs, velocity):
     vmem = pl.BlockSpec(memory_space=pltpu.VMEM)
-    hbm = pl.BlockSpec(memory_space=pl.ANY)
+    hbm = pl.BlockSpec(memory_space=pltpu.HBM)
     npy, npz, ng = pn.npy, pn.npz, fs.ng
     dma = lambda *n: pltpu.SemaphoreType.DMA(n)
     return pl.pallas_call(

time: 54.5 us -> 49.4 us (0.906)
  Pallas kernels: 49.3 us -> 43.7 us
    pallas_call x1, Pallas kernels: 49.3 us -> 43.7 us  [fused(): pl.pallas_call(functools.partial(fused_kernel, pn, fs), in_specs=[hbm] *...]
where the time goes in v2:
time: 49.4 us; the launch traced here: 49 us
  Pallas kernels  43.7 us (88%)
  local copies, waits for them, and re-layouts  4.66 us (9%)
  between operations  0.65 us (1%)
    pallas_call x1, Pallas kernels, fused(): pl.pallas_call(functools.partial(fused_kernel, pn, fs), in_specs=[hbm] *...  43.7 us
    unnamed x8, local copies, waits for them, and re-layouts  4.66 us

profile of v2, /device:TPU:0, one launch (start us, length us, event | category | flops | bytes accessed | tf_op | source)
XLA Modules:
  0.0 49.0 jit_solution(5050538057052243010)
XLA Ops:
  0.6 0.0 copy-start
  0.6 1.4 %copy-done = bf16[3072,256]{1,0:T(8,128)(2,1)S(1)} copy-done((bf16[3072,256]{1,0:T(8,128)(2,1)S(1)}, bf16[3072,256]{1,0:T(8,128)(2,1)}, u32[]{:S(2)}) %copy-start) | copy-done | bytes 1572888
  2.0 0.0 copy-start.1
  2.0 0.9 %copy-done.1 = f32[4,3,8,480]{3,2,1,0:T(8,128)S(1)} copy-done((f32[4,3,8,480]{3,2,1,0:T(8,128)S(1)}, f32[4,3,8,480]{3,2,1,0:T(8,128)}, u32[]{:S(2)}) %copy-start.1) | copy-done | bytes 184344
  3.0 0.0 copy-start.2
  3.0 0.9 %copy-done.2 = f32[8,8,480]{2,1,0:T(8,128)S(1)} copy-done((f32[8,8,480]{2,1,0:T(8,128)S(1)}, f32[8,8,480]{2,1,0:T(8,128)}, u32[]{:S(2)}) %copy-start.2) | copy-done | bytes 122904
  3.9 43.7 %shard_map.59 = (f32[3,32,4,32]{3,2,1,0:T(4,128)S(1)}, f32[6,32,4,32]{3,2,1,0:T(4,128)S(1)}) custom-call(f32[3,20,72,2048]{3,2,1,0:T(8,128)} %bitcast.1, f32[4,3,8,480]{3,2,1,0:T(8,128)S(1)} %copy-done.1, f32[8,8,480]{2,1,0:T(8,128)S(1)} %copy-done.2, bf16[3072,256]{1,0:T(8,128)(2,1)S(1)} %copy-done), custom_call_target="tpu_custom_call" | custom-call | tf_op jit(solution)/shard_map/pallas_call | solution.py:490
  47.6 0.7 %copy.8 = f32[3,32,4,32]{3,2,1,0:T(4,128)} copy(f32[3,32,4,32]{3,2,1,0:T(4,128)S(1)} %get-tuple-element.4) | data formatting | bytes 98304
  48.3 0.7 %copy.9 = f32[6,32,4,32]{3,2,1,0:T(4,128)} copy(f32[6,32,4,32]{3,2,1,0:T(4,128)S(1)} %get-tuple-element.5) | data formatting | bytes 196608
Async XLA Ops:
  0.6 1.4 %copy-start = (bf16[3072,256]{1,0:T(8,128)(2,1)S(1)}, bf16[3072,256]{1,0:T(8,128)(2,1)}, u32[]{:S(2)}) copy-start(bf16[3072,256]{1,0:T(8,128)(2,1)} %constant.8.clone.wx_hbm) | copy-start | bytes 4718596
  2.0 0.9 %copy-start.1 = (f32[4,3,8,480]{3,2,1,0:T(8,128)S(1)}, f32[4,3,8,480]{3,2,1,0:T(8,128)}, u32[]{:S(2)}) copy-start(f32[4,3,8,480]{3,2,1,0:T(8,128)} %constant.6.clone.az_hbm) | copy-start | bytes 552964
  3.0 0.9 %copy-start.2 = (f32[8,8,480]{2,1,0:T(8,128)S(1)}, f32[8,8,480]{2,1,0:T(8,128)}, u32[]{:S(2)}) copy-start(f32[8,8,480]{2,1,0:T(8,128)} %constant.7.clone.ay_hbm) | copy-start | bytes 368644

commit v3 on v2

--- a/solution.py
+++ b/solution.py
@@ -264,36 +264,51 @@
         self.ok = self.ok and min(first) >= 0 and max(first) + (self.nch - 1) * self.cz // 8 + self.nic <= self.slots
         if not self.ok:
             return
-        z0 = np.array([[pn.zl * p + self.cz * c for c in range(self.nch)] for p in range(npz)])
-        z = z0[:, :, None, None] + np.arange(self.cz)
-        i = (z0 // 8 - 4)[:, :, None, None] + np.arange(self.nic)[:, None]
-        az = np.where((i >= 0) & (i < pn.oz), tap(z - 16 - 8 * i), 0.0)
-        az = np.pad(az, ((0, 0), (0, 0), (0, -self.nic % 8), (0, 0)))
-        self.az = np.tile(az, (1, 1, 1, pn.yl)).astype(np.float32)
-        ay = np.zeros((npy, 8, pn.yl))
-        for d in range(npy):
-            for j in range(pn.oy):
-                w = tap(pn.yl * d + np.arange(pn.yl) - 16 - 8 * j)
-                if np.any(w != 0):
-                    ay[d, j % 8] += w
-        self.ay = np.repeat(ay, self.cz, axis=2).astype(np.float32)
-        n = np.arange(self.xt)[:, None]
-        k = np.arange(32)[None, :]
-        main = tap(n - 8 * k)
-        edge = np.where(k >= 16, tap(n - 8 * k + self.xt), tap(n - 8 * k - self.xt))
-        wx = np.concatenate([main, edge], axis=1).astype(np.float32)
-        hi = wx.astype(ml_dtypes.bfloat16)
-        lo = (wx - hi.astype(np.float32)).astype(ml_dtypes.bfloat16)
-        t = np.zeros((4, 3, self.xt, 2, 4, 32), ml_dtypes.bfloat16)
-        for q in range(4):
-            for n, val in enumerate((hi, hi, lo)):
-                t[q, n, :, :, q] = val.reshape(self.xt, 2, 32)
-        self.wx = t.reshape(12 * self.xt, 256)
-
-
-def fused_kernel(pn, fs, v_hbm, az_hbm, ay_hbm, wx_hbm, vel_ref, str_ref,
-                 vbuf, az, ay, wx, w2, acc, part, rec_h, rec_y, snd_z, rec_z,
-                 sv, st, sh, rh, sy, ry, sz, rz):
+
+
+def taps(t):
+    r = np.arange(-16, 17).astype(np.float64)
+    scale = float(1.0 / np.sum(np.exp(-r * r / 128.0)))
+    val = jnp.exp((t * t).astype(f32) * (-1.0 / 128.0)) * scale
+    return jnp.where((t >= -16) & (t <= 16), val, 0.0)
+
+
+def weights(pn, fs, d, p, w2, wx):
+    iota = lax.broadcasted_iota
+    nic, cz, xt = fs.nic, fs.cz, fs.xt
+    m = nic * 8
+    col = iota(jnp.int32, (8, fs.kk), 1)
+    slot = iota(jnp.int32, (8, fs.kk), 0)
+    y = jnp.floor((col.astype(f32) + 0.5) * (1.0 / cz)).astype(jnp.int32)
+    z = col - y * cz
+    wy = jnp.zeros((8, fs.kk), f32)
+    for h in range(pn.oy // 8):
+        wy = wy + taps(pn.yl * d + y - 16 - 8 * (slot + 8 * h))
+    wz0 = taps(z + 16 - 8 * slot)
+    for c in range(fs.nch):
+        i = (pn.zl * p + cz * c) // 8 - 4 + slot
+        wz = jnp.where((i >= 0) & (i < pn.oz), wz0, 0.0)[:nic]
+        w = (wz[:, None, :] * wy[None, :, :]).reshape(m, fs.kk)
+        w_hi = w.astype(bf16).astype(f32)
+        w2[c, :m] = w_hi
+        w2[c, m:] = w - w_hi
+    row = iota(jnp.int32, (xt, 128), 0)
+    lane = iota(jnp.int32, (xt, 128), 1)
+    k = lane & 31
+    t = row - 8 * k
+    main = taps(t)
+    edge = taps(jnp.where(k >= 16, t + xt, t - xt))
+    for q in range(4):
+        here = (lane >> 5) == q
+        val = jnp.concatenate([jnp.where(here, main, 0.0), jnp.where(here, edge, 0.0)], axis=1)
+        hi, lo = split(val)
+        for n, part in enumerate((hi, hi, lo)):
+            wx[(3 * q + n) * xt:(3 * q + n + 1) * xt] = part
+
+
+def fused_kernel(pn, fs, v_hbm, vel_ref, str_ref,
+                 vbuf, wx, w2, acc, part, rec_h, rec_d, rec_y, snd_z, rec_z,
+                 sv, sh, rh, sd, rd, sy, ry, sz, rz):
     d, p = lax.axis_index("py"), lax.axis_index("pz")
     npy, npz, jq, kb = pn.npy, pn.npz, pn.jq, pn.kb
     xt, cz, nch, nic, groups, ng = fs.xt, fs.cz, fs.nch, fs.nic, fs.groups, fs.ng
@@ -306,30 +321,17 @@
             v_hbm.at[:, :, pl.ds(c * cz, cz), pl.ds(x, xt)],
             vbuf.at[b, :, :, pl.ds(c * cz, cz), :], sv.at[b, c])
 
-    tables = [pltpu.make_async_copy(az_hbm.at[p], az, st.at[0]),
-              pltpu.make_async_copy(ay_hbm.at[d], ay, st.at[1]),
-              pltpu.make_async_copy(wx_hbm, wx, st.at[2])]
-    for t in tables:
-        t.start()
     for c in range(nch):
         load(0, c).start()
 
     barrier = pltpu.get_barrier_semaphore()
-    for o in range(1, npy):
-        pl.semaphore_signal(barrier, inc=1, device_id=(lax.rem(d + o, npy), p), device_id_type=mesh_id)
-    for o in range(1, npz):
-        pl.semaphore_signal(barrier, inc=1, device_id=(d, lax.rem(p + o, npz)), device_id_type=mesh_id)
+    for o in range(1, npy * npz):
+        od, op = divmod(o, npz)
+        to = (lax.rem(d + od, npy), lax.rem(p + op, npz))
+        pl.semaphore_signal(barrier, inc=1, device_id=to, device_id_type=mesh_id)
 
     part[...] = jnp.zeros_like(part)
-    for t in tables:
-        t.wait()
-    for c in range(nch):
-        wz = az[c][:nic]
-        w = (wz[:, None, :] * ay[...][None, :, :]).reshape(nic * 8, fs.kk)
-        w_hi = w.astype(bf16)
-        w2[c, :nic * 8] = w_hi.astype(f32)
-        w2[c, nic * 8:] = w - w_hi.astype(f32)
-    pl.semaphore_wait(barrier, npy + npz - 2)
+    weights(pn, fs, d, p, w2, wx)
 
     sub = lax.rem(lax.broadcasted_iota(jnp.int32, (groups, 9, 8, 128), 3), 32)
     m = nic * 8
@@ -348,6 +350,13 @@
         return pltpu.make_async_remote_copy(
             src_ref=part.at[b, pl.ds(1, ng)], dst_ref=rec_y.at[d], send_sem=sy.at[b], recv_sem=ry.at[b],
             device_id=(lax.rem(d + b, npy), p), device_id_type=mesh_id)
+
+    def slant(b, k):
+        o = b - (npy - 2)
+        to = (lax.rem(d + b, npy), lax.rem(p + (1 if k == 0 else npz - 1), npz))
+        return pltpu.make_async_remote_copy(
+            src_ref=part.at[b, groups - 1 if k == 0 else 0], dst_ref=rec_d.at[o, k], send_sem=sd.at[o, k],
+            recv_sem=rd.at[o, k], device_id=to, device_id_type=mesh_id)
 
     def halo_start(b):
         @pl.when(p < npz - 1)
@@ -423,28 +432,38 @@
         part[left] += jnp.where(sub >= 16, edge, 0.0)
         part[right] += jnp.where(sub < 16, edge, 0.0)
 
+        @pl.when(s == 1)
+        def _():
+            pl.semaphore_wait(barrier, npy * npz - 1)
+
         @pl.when(s >= 3)
         def _():
             halo_finish(s - 2)
             across(s - 2).start()
 
-        @pl.when(s >= 2)
+        @pl.when((s >= 2) & (s <= npy - 2))
         def _():
             halo_start(s - 1)
         return carry
 
     lax.fori_loop(0, npy, block, 0)
-    halo_start(npy - 1)
+    late = [(o, k) for o in (npy - 2, npy - 1) for k in range(2)]
+    for o in (npy - 2, npy - 1):
+        across(o).start()
+    for o, k in late:
+        @pl.when((p < npz - 1) if k == 0 else (p > 0))
+        def _():
+            slant(o, k).start()
     halo_start(0)
-    for o in (npy - 2, npy - 1):
-        halo_finish(o)
-        across(o).start()
     halo_finish(0)
     rec_y[d] = part[0, 1:1 + ng]
     for o in range(1, npy):
         across(o).wait()
-    for o in range(npy):
-        halo_sent(o)
+    for o, k in late:
+        @pl.when((p > 0) if k == 0 else (p < npz - 1))
+        def _():
+            slant(o, k).wait_recv()
+            rec_y[lax.rem(d + npy - o, npy), 0 if k == 0 else ng - 1] += rec_d[o - (npy - 2), k]
 
     rowi = lax.broadcasted_iota(jnp.int32, (ng, 9, 8, 128), 2)
     for h in range(pn.oy // 8):
@@ -470,6 +489,12 @@
     rec_z[p] = snd_z[p]
     for copy in copies:
         copy.wait()
+    for o in range(npy - 2):
+        halo_sent(o)
+    for o, k in late:
+        @pl.when((p < npz - 1) if k == 0 else (p > 0))
+        def _():
+            slant(o, k).wait_send()
     for s in range(npz):
         for g in range(ng):
             t = rec_z[s, g]
@@ -489,27 +514,26 @@
     dma = lambda *n: pltpu.SemaphoreType.DMA(n)
     return pl.pallas_call(
         functools.partial(fused_kernel, pn, fs),
-        in_specs=[hbm] * 4,
+        in_specs=[hbm],
         out_specs=(vmem, vmem),
         out_shape=tuple(jax.ShapeDtypeStruct((n, pn.oz, pn.jq, pn.kb), f32) for n in (3, 6)),
         scratch_shapes=[
             pltpu.VMEM((2, 3, pn.yl, pn.zl, fs.xt), f32),
-            pltpu.VMEM(fs.az.shape[1:], f32),
-            pltpu.VMEM(fs.ay.shape[1:], f32),
-            pltpu.VMEM(fs.wx.shape, bf16),
+            pltpu.VMEM((12 * fs.xt, 256), bf16),
             pltpu.VMEM((fs.nch, 2 * fs.nic * 8, fs.kk), f32),
             pltpu.VMEM((9, fs.slots, 8, fs.xt), f32),
             pltpu.VMEM((npy, fs.groups, 9, 8, 128), f32),
             pltpu.VMEM((npy, 2, 9, 8, 128), f32),
+            pltpu.VMEM((2, 2, 9, 8, 128), f32),
             pltpu.VMEM((npy, ng, 9, 8, 128), f32),
             pltpu.VMEM((npz, ng, 9, pn.jq, 128), f32),
             pltpu.VMEM((npz, ng, 9, pn.jq, 128), f32),
-            dma(2, fs.nch), dma(3), dma(npy, 2), dma(npy, 2), dma(npy), dma(npy), dma(npz), dma(npz),
+            dma(2, fs.nch), dma(npy, 2), dma(npy, 2), dma(2, 2), dma(2, 2), dma(npy), dma(npy), dma(npz), dma(npz),
         ],
         compiler_params=pltpu.CompilerParams(
             collective_id=0, has_side_effects=True, vmem_limit_bytes=50 * 2**20
         ),
-    )(velocity, *[jnp.asarray(t) for t in (fs.az, fs.ay, fs.wx)])
+    )(velocity)
 
 
 def on_device(npy, npz, velocity):

time: 49.4 us -> 46.6 us (0.943)
  the two profiles are of different devices: /device:TPU:0 before, /device:TPU:15 now
where the time goes in v3:
time: 46.6 us; the launch traced here: 46.5 us
  Pallas kernels  44.4 us (95%)
  local copies, waits for them, and re-layouts  1.42 us (3%)
  between operations  0.64 us (1%)
    pallas_call x1, Pallas kernels, fused(): pl.pallas_call(functools.partial(fused_kernel, pn, fs), in_specs=[hbm], o...  44.4 us
    unnamed x2, local copies, waits for them, and re-layouts  1.42 us

profile of v3, /device:TPU:15, one launch (start us, length us, event | category | flops | bytes accessed | tf_op | source)
XLA Modules:
  0.0 46.5 jit_solution(9682077334848525696)
XLA Ops:
  0.6 44.4 %shard_map.30 = (f32[3,32,4,32]{3,2,1,0:T(4,128)S(1)}, f32[6,32,4,32]{3,2,1,0:T(4,128)S(1)}) custom-call(f32[3,20,72,2048]{3,2,1,0:T(8,128)} %bitcast.1), custom_call_target="tpu_custom_call" | custom-call | tf_op jit(solution)/shard_map/pallas_call | solution.py:515
  45.1 0.7 %copy.5 = f32[3,32,4,32]{3,2,1,0:T(4,128)} copy(f32[3,32,4,32]{3,2,1,0:T(4,128)S(1)} %get-tuple-element.4) | data formatting | bytes 98304
  45.7 0.7 %copy.6 = f32[6,32,4,32]{3,2,1,0:T(4,128)} copy(f32[6,32,4,32]{3,2,1,0:T(4,128)S(1)} %get-tuple-element.5) | data formatting | bytes 196608

commit v4 on v3

--- a/solution.py
+++ b/solution.py
@@ -261,7 +261,11 @@
         self.first = first
         self.step = first[1] - first[0]
         self.ok = all(f == first[0] + self.step * p for p, f in enumerate(first))
-        self.ok = self.ok and min(first) >= 0 and max(first) + (self.nch - 1) * self.cz // 8 + self.nic <= self.slots
+        y0 = pn.yl * np.arange(npy)
+        self.jlo = [int(max(0, (y + 7) // 8 - 4)) for y in y0]
+        self.rows = [int(min(pn.oy - 1, (y + pn.yl - 1) // 8)) - j + 1 for y, j in zip(y0, self.jlo)]
+        self.sent = [min(8, n | 1) for n in self.rows]
+        self.ok = self.ok and 0 < min(self.rows) and max(self.rows) <= 8 and min(first) >= 0 and max(first) + (self.nch - 1) * self.cz // 8 + self.nic <= self.slots
         if not self.ok:
             return
 
@@ -281,9 +285,8 @@
     slot = iota(jnp.int32, (8, fs.kk), 0)
     y = jnp.floor((col.astype(f32) + 0.5) * (1.0 / cz)).astype(jnp.int32)
     z = col - y * cz
-    wy = jnp.zeros((8, fs.kk), f32)
-    for h in range(pn.oy // 8):
-        wy = wy + taps(pn.yl * d + y - 16 - 8 * (slot + 8 * h))
+    j = jnp.maximum((pn.yl * d + 7) // 8 - 4, 0) + slot
+    wy = jnp.where(j < pn.oy, taps(pn.yl * d + y - 16 - 8 * j), 0.0)
     wz0 = taps(z + 16 - 8 * slot)
     for c in range(fs.nch):
         i = (pn.zl * p + cz * c) // 8 - 4 + slot
@@ -307,7 +310,7 @@
 
 
 def fused_kernel(pn, fs, v_hbm, vel_ref, str_ref,
-                 vbuf, wx, w2, acc, part, rec_h, rec_d, rec_y, snd_z, rec_z,
+                 vbuf, wx, w2, acc, part, rec_h, rec_d, rec_y, tot, snd_z, rec_z,
                  sv, sh, rh, sd, rd, sy, ry, sz, rz):
     d, p = lax.axis_index("py"), lax.axis_index("pz")
     npy, npz, jq, kb = pn.npy, pn.npz, pn.jq, pn.kb
@@ -315,7 +318,7 @@
     mesh_id = pl.DeviceIdType.MESH
 
     def load(s, c):
-        x = pl.multiple_of(lax.rem(d + s, npy) * xt, xt)
+        x = pl.multiple_of(lax.rem(d + 1 + s, npy) * xt, xt)
         b = lax.rem(s, 2)
         return pltpu.make_async_copy(
             v_hbm.at[:, :, pl.ds(c * cz, cz), pl.ds(x, xt)],
@@ -346,17 +349,25 @@
             src_ref=part.at[b, 0], dst_ref=rec_h.at[b, 1], send_sem=sh.at[b, 1], recv_sem=rh.at[b, 1],
             device_id=(d, lax.rem(p + npz - 1, npz)), device_id_type=mesh_id)
 
-    def across(b):
+    def across(b, n):
         return pltpu.make_async_remote_copy(
-            src_ref=part.at[b, pl.ds(1, ng)], dst_ref=rec_y.at[d], send_sem=sy.at[b], recv_sem=ry.at[b],
-            device_id=(lax.rem(d + b, npy), p), device_id_type=mesh_id)
-
-    def slant(b, k):
-        o = b - (npy - 2)
-        to = (lax.rem(d + b, npy), lax.rem(p + (1 if k == 0 else npz - 1), npz))
+            src_ref=part.at[b, pl.ds(1, ng), :, pl.ds(0, n)], dst_ref=rec_y.at[d, :, :, pl.ds(0, n)],
+            send_sem=sy.at[b], recv_sem=ry.at[b], device_id=(lax.rem(d + 1 + b, npy), p), device_id_type=mesh_id)
+
+    def slant(b, k, n):
+        o = 1 if b else 0
+        to = (lax.rem(d + 1 + b, npy), lax.rem(p + (1 if k == 0 else npz - 1), npz))
         return pltpu.make_async_remote_copy(
-            src_ref=part.at[b, groups - 1 if k == 0 else 0], dst_ref=rec_d.at[o, k], send_sem=sd.at[o, k],
-            recv_sem=rd.at[o, k], device_id=to, device_id_type=mesh_id)
+            src_ref=part.at[b, groups - 1 if k == 0 else 0, :, pl.ds(0, n)], dst_ref=rec_d.at[o, k, :, pl.ds(0, n)],
+            send_sem=sd.at[o, k], recv_sem=rd.at[o, k], device_id=to, device_id_type=mesh_id)
+
+    def by_rows(who, act):
+        for n in sorted(set(fs.sent)):
+            mine = [who == i for i in range(npy) if fs.sent[i] == n]
+
+            @pl.when(functools.reduce(jnp.logical_or, mine))
+            def _():
+                act(n)
 
     def halo_start(b):
         @pl.when(p < npz - 1)
@@ -439,7 +450,7 @@
         @pl.when(s >= 3)
         def _():
             halo_finish(s - 2)
-            across(s - 2).start()
+            by_rows(d, lambda n: across(s - 2, n).start())
 
         @pl.when((s >= 2) & (s <= npy - 2))
         def _():
@@ -447,37 +458,41 @@
         return carry
 
     lax.fori_loop(0, npy, block, 0)
-    late = [(o, k) for o in (npy - 2, npy - 1) for k in range(2)]
-    for o in (npy - 2, npy - 1):
-        across(o).start()
-    for o, k in late:
-        @pl.when((p < npz - 1) if k == 0 else (p > 0))
-        def _():
-            slant(o, k).start()
-    halo_start(0)
-    halo_finish(0)
-    rec_y[d] = part[0, 1:1 + ng]
-    for o in range(1, npy):
-        across(o).wait()
-    for o, k in late:
-        @pl.when((p > 0) if k == 0 else (p < npz - 1))
-        def _():
-            slant(o, k).wait_recv()
-            rec_y[lax.rem(d + npy - o, npy), 0 if k == 0 else ng - 1] += rec_d[o - (npy - 2), k]
-
-    rowi = lax.broadcasted_iota(jnp.int32, (ng, 9, 8, 128), 2)
-    for h in range(pn.oy // 8):
-        total = jnp.zeros((ng, 9, 8, 128), f32)
-        for s in range(npy):
-            rows = np.nonzero(pn.mask[s, h])[0]
-            if len(rows) == 0:
-                continue
-            val = rec_y[s]
-            if len(rows) < 8:
-                val = jnp.where((rowi >= int(rows[0])) & (rowi <= int(rows[-1])), val, 0.0)
-            total = total + val
-        for q in range(8 // jq):
-            snd_z[h * (8 // jq) + q] = total[:, :, q * jq:(q + 1) * jq, :]
+    own = npy - 1
+    has_up, has_down = p < npz - 1, p > 0
+
+    def late_start(n):
+        for b in (npy - 2, 0):
+            across(b, n).start()
+            for k in range(2):
+                @pl.when((has_up, has_down)[k])
+                def _():
+                    slant(b, k, n).start()
+
+    by_rows(d, late_start)
+    halo_start(own)
+    halo_finish(own)
+    rec_y[d] = part[own, 1:1 + ng]
+    for b in list(range(1, npy - 1)) + [0]:
+        src = lax.rem(d + 2 * npy - 1 - b, npy)
+
+        def arrive(n):
+            across(b, n).wait_recv()
+            if b in (npy - 2, 0):
+                for k in range(2):
+                    @pl.when((has_down, has_up)[k])
+                    def _():
+                        slant(b, k, n).wait_recv()
+                        rec_y[src, 0 if k == 0 else ng - 1] += rec_d[1 if b else 0, k]
+
+        by_rows(src, arrive)
+
+    tot[...] = jnp.zeros_like(tot)
+    for s in range(npy):
+        j, n = fs.jlo[s], fs.rows[s]
+        tot[:, :, j:j + n, :] += rec_y[s, :, :, 0:n, :]
+    for q in range(npz):
+        snd_z[q] = tot[:, :, q * jq:(q + 1) * jq, :]
     copies = []
     for o in range(1, npz):
         to = lax.rem(p + o, npz)
@@ -489,12 +504,19 @@
     rec_z[p] = snd_z[p]
     for copy in copies:
         copy.wait()
-    for o in range(npy - 2):
-        halo_sent(o)
-    for o, k in late:
-        @pl.when((p < npz - 1) if k == 0 else (p > 0))
-        def _():
-            slant(o, k).wait_send()
+    for b in list(range(1, npy - 2)) + [own]:
+        halo_sent(b)
+
+    def sent(n):
+        for b in range(npy - 1):
+            across(b, n).wait_send()
+        for b in (npy - 2, 0):
+            for k in range(2):
+                @pl.when((has_up, has_down)[k])
+                def _():
+                    slant(b, k, n).wait_send()
+
+    by_rows(d, sent)
     for s in range(npz):
         for g in range(ng):
             t = rec_z[s, g]
@@ -526,6 +548,7 @@
             pltpu.VMEM((npy, 2, 9, 8, 128), f32),
             pltpu.VMEM((2, 2, 9, 8, 128), f32),
             pltpu.VMEM((npy, ng, 9, 8, 128), f32),
+            pltpu.VMEM((ng, 9, pn.oy, 128), f32),
             pltpu.VMEM((npz, ng, 9, pn.jq, 128), f32),
             pltpu.VMEM((npz, ng, 9, pn.jq, 128), f32),
             dma(2, fs.nch), dma(npy, 2), dma(npy, 2), dma(2, 2), dma(2, 2), dma(npy), dma(npy), dma(npz), dma(npz),

time: 46.6 us -> 43.9 us (0.942)
  the two profiles are of different devices: /device:TPU:15 before, /device:TPU:0 now
where the time goes in v4:
time: 43.9 us; the launch traced here: 43.7 us
  Pallas kernels  41.7 us (95%)
  local copies, waits for them, and re-layouts  1.42 us (3%)
  between operations  0.64 us (1%)
    pallas_call x1, Pallas kernels, fused(): pl.pallas_call(functools.partial(fused_kernel, pn, fs), in_specs=[hbm], o...  41.7 us
    unnamed x2, local copies, waits for them, and re-layouts  1.42 us

profile of v4, /device:TPU:0, one launch (start us, length us, event | category | flops | bytes accessed | tf_op | source)
XLA Modules:
  0.0 43.7 jit_solution(15665505472375264193)
XLA Ops:
  0.6 41.7 %shard_map.30 = (f32[3,32,4,32]{3,2,1,0:T(4,128)S(1)}, f32[6,32,4,32]{3,2,1,0:T(4,128)S(1)}) custom-call(f32[3,20,72,2048]{3,2,1,0:T(8,128)} %bitcast.1), custom_call_target="tpu_custom_call" | custom-call | tf_op jit(solution)/shard_map/pallas_call | solution.py:537
  42.3 0.7 %copy.5 = f32[3,32,4,32]{3,2,1,0:T(4,128)} copy(f32[3,32,4,32]{3,2,1,0:T(4,128)S(1)} %get-tuple-element.4) | data formatting | bytes 98304
  43.0 0.7 %copy.6 = f32[6,32,4,32]{3,2,1,0:T(4,128)} copy(f32[6,32,4,32]{3,2,1,0:T(4,128)S(1)} %get-tuple-element.5) | data formatting | bytes 196608

commit v5 on v4

--- a/solution.py
+++ b/solution.py
@@ -411,14 +411,14 @@
             load(s, c).wait()
             wt = w2[c].astype(bf16)
             row = fs.first[0] + fs.step * p + c * (cz // 8)
-            for f in range(9):
+            for n, f in enumerate((0, 3, 4, 1, 6, 7, 2, 8, 5)):
                 if f < 3:
                     val = vbuf[b, f, :, c * cz:(c + 1) * cz, :]
                 else:
                     a1, a2 = stress_pairs[f - 3]
                     val = vbuf[b, a1, :, c * cz:(c + 1) * cz, :] * vbuf[b, a2, :, c * cz:(c + 1) * cz, :]
                 hi, lo = split(val.reshape(fs.kk, xt))
-                if f % 2 == 0:
+                if n % 2 == 0:
                     r = dot(wt, hi)
                     r = r[:m] + r[m:] + dot(wt[:m], lo)
                 else:

time: 43.9 us -> 43 us (0.979)
  Pallas kernels: 41.7 us -> 40.8 us
    pallas_call x1, Pallas kernels: 41.7 us -> 40.8 us  [fused(): pl.pallas_call(functools.partial(fused_kernel, pn, fs), in_specs=[hbm], o...]
where the time goes in v5:
time: 43 us; the launch traced here: 42.9 us
  Pallas kernels  40.8 us (95%)
  local copies, waits for them, and re-layouts  1.42 us (3%)
  between operations  0.64 us (1%)
    pallas_call x1, Pallas kernels, fused(): pl.pallas_call(functools.partial(fused_kernel, pn, fs), in_specs=[hbm], o...  40.8 us
    unnamed x2, local copies, waits for them, and re-layouts  1.42 us

profile of v5, /device:TPU:0, one launch (start us, length us, event | category | flops | bytes accessed | tf_op | source)
XLA Modules:
  0.0 42.9 jit_solution(8754618112606431056)
XLA Ops:
  0.6 40.8 %shard_map.30 = (f32[3,32,4,32]{3,2,1,0:T(4,128)S(1)}, f32[6,32,4,32]{3,2,1,0:T(4,128)S(1)}) custom-call(f32[3,20,72,2048]{3,2,1,0:T(8,128)} %bitcast.1), custom_call_target="tpu_custom_call" | custom-call | tf_op jit(solution)/shard_map/pallas_call | solution.py:537
  41.4 0.7 %copy.5 = f32[3,32,4,32]{3,2,1,0:T(4,128)} copy(f32[3,32,4,32]{3,2,1,0:T(4,128)S(1)} %get-tuple-element.4) | data formatting | bytes 98304
  42.1 0.7 %copy.6 = f32[6,32,4,32]{3,2,1,0:T(4,128)} copy(f32[6,32,4,32]{3,2,1,0:T(4,128)S(1)} %get-tuple-element.5) | data formatting | bytes 196608

commit v6 on v5

--- a/solution.py
+++ b/solution.py
@@ -277,7 +277,7 @@
     return jnp.where((t >= -16) & (t <= 16), val, 0.0)
 
 
-def weights(pn, fs, d, p, w2, wx):
+def weights(pn, fs, d, p, w2, w1, wx):
     iota = lax.broadcasted_iota
     nic, cz, xt = fs.nic, fs.cz, fs.xt
     m = nic * 8
@@ -293,8 +293,8 @@
         wz = jnp.where((i >= 0) & (i < pn.oz), wz0, 0.0)[:nic]
         w = (wz[:, None, :] * wy[None, :, :]).reshape(m, fs.kk)
         w_hi = w.astype(bf16).astype(f32)
-        w2[c, :m] = w_hi
-        w2[c, m:] = w - w_hi
+        w2[c] = jnp.concatenate([w_hi, w - w_hi], axis=0).astype(bf16)
+        w1[c] = jnp.concatenate([w_hi, jnp.zeros((w1.shape[1] - m, fs.kk), f32)], axis=0).astype(bf16)
     row = iota(jnp.int32, (xt, 128), 0)
     lane = iota(jnp.int32, (xt, 128), 1)
     k = lane & 31
@@ -310,7 +310,7 @@
 
 
 def fused_kernel(pn, fs, v_hbm, vel_ref, str_ref,
-                 vbuf, wx, w2, acc, part, rec_h, rec_d, rec_y, tot, snd_z, rec_z,
+                 vbuf, wx, w2, w1, acc, part, rec_h, rec_d, rec_y, tot, snd_z, rec_z,
                  sv, sh, rh, sd, rd, sy, ry, sz, rz):
     d, p = lax.axis_index("py"), lax.axis_index("pz")
     npy, npz, jq, kb = pn.npy, pn.npz, pn.jq, pn.kb
@@ -334,7 +334,7 @@
         pl.semaphore_signal(barrier, inc=1, device_id=to, device_id_type=mesh_id)
 
     part[...] = jnp.zeros_like(part)
-    weights(pn, fs, d, p, w2, wx)
+    weights(pn, fs, d, p, w2, w1, wx)
 
     sub = lax.rem(lax.broadcasted_iota(jnp.int32, (groups, 9, 8, 128), 3), 32)
     m = nic * 8
@@ -409,7 +409,7 @@
         acc[...] = jnp.zeros_like(acc)
         for c in range(nch):
             load(s, c).wait()
-            wt = w2[c].astype(bf16)
+            wt, wt_hi = w2[c], w1[c]
             row = fs.first[0] + fs.step * p + c * (cz // 8)
             for n, f in enumerate((0, 3, 4, 1, 6, 7, 2, 8, 5)):
                 if f < 3:
@@ -418,11 +418,11 @@
                     a1, a2 = stress_pairs[f - 3]
                     val = vbuf[b, a1, :, c * cz:(c + 1) * cz, :] * vbuf[b, a2, :, c * cz:(c + 1) * cz, :]
                 hi, lo = split(val.reshape(fs.kk, xt))
-                if n % 2 == 0:
+                if (n + c) % 2 == 0:
                     r = dot(wt, hi)
-                    r = r[:m] + r[m:] + dot(wt[:m], lo)
+                    r = r[:m] + r[m:] + dot(wt_hi, lo)[:m]
                 else:
-                    r_lo = dot(wt[:m], lo)
+                    r_lo = dot(wt_hi, lo)[:m]
                     r = dot(wt, hi)
                     r = r[:m] + r[m:] + r_lo
                 acc[f, pl.ds(row, nic)] += r.reshape(nic, 8, xt)
@@ -542,7 +542,8 @@
         scratch_shapes=[
             pltpu.VMEM((2, 3, pn.yl, pn.zl, fs.xt), f32),
             pltpu.VMEM((12 * fs.xt, 256), bf16),
-            pltpu.VMEM((fs.nch, 2 * fs.nic * 8, fs.kk), f32),
+            pltpu.VMEM((fs.nch, 2 * fs.nic * 8, fs.kk), bf16),
+            pltpu.VMEM((fs.nch, -(-fs.nic // 2) * 16, fs.kk), bf16),
             pltpu.VMEM((9, fs.slots, 8, fs.xt), f32),
             pltpu.VMEM((npy, fs.groups, 9, 8, 128), f32),
             pltpu.VMEM((npy, 2, 9, 8, 128), f32),

time: 43 us -> 43 us (level)
  no operation moved by 1% of the time
where the time goes in v6:
time: 43 us; the launch traced here: 42.8 us
  Pallas kernels  40.8 us (95%)
  local copies, waits for them, and re-layouts  1.42 us (3%)
  between operations  0.64 us (1%)
    pallas_call x1, Pallas kernels, fused(): pl.pallas_call(functools.partial(fused_kernel, pn, fs), in_specs=[hbm], o...  40.8 us
    unnamed x2, local copies, waits for them, and re-layouts  1.42 us

profile of v6, /device:TPU:0, one launch (start us, length us, event | category | flops | bytes accessed | tf_op | source)
XLA Modules:
  0.0 42.8 jit_solution(1049821098091076741)
XLA Ops:
  0.6 40.8 %shard_map.30 = (f32[3,32,4,32]{3,2,1,0:T(4,128)S(1)}, f32[6,32,4,32]{3,2,1,0:T(4,128)S(1)}) custom-call(f32[3,20,72,2048]{3,2,1,0:T(8,128)} %bitcast.1), custom_call_target="tpu_custom_call" | custom-call | tf_op jit(solution)/shard_map/pallas_call | solution.py:537
  41.4 0.7 %copy.5 = f32[3,32,4,32]{3,2,1,0:T(4,128)} copy(f32[3,32,4,32]{3,2,1,0:T(4,128)S(1)} %get-tuple-element.4) | data formatting | bytes 98304
  42.1 0.7 %copy.6 = f32[6,32,4,32]{3,2,1,0:T(4,128)} copy(f32[6,32,4,32]{3,2,1,0:T(4,128)S(1)} %get-tuple-element.5) | data formatting | bytes 196608

commit v7 on v5

--- a/solution.py
+++ b/solution.py
@@ -264,7 +264,7 @@
         y0 = pn.yl * np.arange(npy)
         self.jlo = [int(max(0, (y + 7) // 8 - 4)) for y in y0]
         self.rows = [int(min(pn.oy - 1, (y + pn.yl - 1) // 8)) - j + 1 for y, j in zip(y0, self.jlo)]
-        self.sent = [min(8, n | 1) for n in self.rows]
+        self.sent = list(self.rows)
         self.ok = self.ok and 0 < min(self.rows) and max(self.rows) <= 8 and min(first) >= 0 and max(first) + (self.nch - 1) * self.cz // 8 + self.nic <= self.slots
         if not self.ok:
             return
@@ -488,22 +488,22 @@
         by_rows(src, arrive)
 
     tot[...] = jnp.zeros_like(tot)
-    for s in range(npy):
-        j, n = fs.jlo[s], fs.rows[s]
-        tot[:, :, j:j + n, :] += rec_y[s, :, :, 0:n, :]
-    for q in range(npz):
-        snd_z[q] = tot[:, :, q * jq:(q + 1) * jq, :]
     copies = []
-    for o in range(1, npz):
-        to = lax.rem(p + o, npz)
-        copy = pltpu.make_async_remote_copy(
-            src_ref=snd_z.at[to], dst_ref=rec_z.at[p], send_sem=sz.at[o], recv_sem=rz.at[o],
-            device_id=(d, to), device_id_type=mesh_id)
-        copy.start()
-        copies.append(copy)
+    for g in range(ng):
+        for s in range(npy):
+            j, n = fs.jlo[s], fs.rows[s]
+            tot[g, :, j:j + n, :] += rec_y[s, g, :, 0:n, :]
+        for q in range(npz):
+            snd_z[q, g] = tot[g, :, q * jq:(q + 1) * jq, :]
+        for o in range(1, npz):
+            to = lax.rem(p + o, npz)
+            copy = pltpu.make_async_remote_copy(
+                src_ref=snd_z.at[to, g], dst_ref=rec_z.at[p, g], send_sem=sz.at[o, g], recv_sem=rz.at[o, g],
+                device_id=(d, to), device_id_type=mesh_id)
+            copy.start()
+            copies.append(copy)
     rec_z[p] = snd_z[p]
-    for copy in copies:
-        copy.wait()
+
     for b in list(range(1, npy - 2)) + [own]:
         halo_sent(b)
 
@@ -517,8 +517,10 @@
                     slant(b, k, n).wait_send()
 
     by_rows(d, sent)
-    for s in range(npz):
-        for g in range(ng):
+    for g in range(ng):
+        for copy in copies[g * (npz - 1):(g + 1) * (npz - 1)]:
+            copy.wait()
+        for s in range(npz):
             t = rec_z[s, g]
             tau = [t[3 + n] - t[a] * t[b] for n, (a, b) in enumerate(stress_pairs)]
             for q in range(4):
@@ -551,7 +553,7 @@
             pltpu.VMEM((ng, 9, pn.oy, 128), f32),
             pltpu.VMEM((npz, ng, 9, pn.jq, 128), f32),
             pltpu.VMEM((npz, ng, 9, pn.jq, 128), f32),
-            dma(2, fs.nch), dma(npy, 2), dma(npy, 2), dma(2, 2), dma(2, 2), dma(npy), dma(npy), dma(npz), dma(npz),
+            dma(2, fs.nch), dma(npy, 2), dma(npy, 2), dma(2, 2), dma(2, 2), dma(npy), dma(npy), dma(npz, ng), dma(npz, ng),
         ],
         compiler_params=pltpu.CompilerParams(
             collective_id=0, has_side_effects=True, vmem_limit_bytes=50 * 2**20

time: 43 us -> 42.8 us (level)
  no operation moved by 1% of the time
where the time goes in v7:
time: 42.8 us; the launch traced here: 42.7 us
  Pallas kernels  40.6 us (95%)
  local copies, waits for them, and re-layouts  1.42 us (3%)
  between operations  0.64 us (1%)
    pallas_call x1, Pallas kernels, fused(): pl.pallas_call(functools.partial(fused_kernel, pn, fs), in_specs=[hbm], o...  40.6 us
    unnamed x2, local copies, waits for them, and re-layouts  1.42 us

profile of v7, /device:TPU:0, one launch (start us, length us, event | category | flops | bytes accessed | tf_op | source)
XLA Modules:
  0.0 42.7 jit_solution(11912398050637519078)
XLA Ops:
  0.6 40.6 %shard_map.30 = (f32[3,32,4,32]{3,2,1,0:T(4,128)S(1)}, f32[6,32,4,32]{3,2,1,0:T(4,128)S(1)}) custom-call(f32[3,20,72,2048]{3,2,1,0:T(8,128)} %bitcast.1), custom_call_target="tpu_custom_call" | custom-call | tf_op jit(solution)/shard_map/pallas_call | solution.py:539
  41.2 0.7 %copy.5 = f32[3,32,4,32]{3,2,1,0:T(4,128)} copy(f32[3,32,4,32]{3,2,1,0:T(4,128)S(1)} %get-tuple-element.4) | data formatting | bytes 98304
  41.9 0.7 %copy.6 = f32[6,32,4,32]{3,2,1,0:T(4,128)} copy(f32[6,32,4,32]{3,2,1,0:T(4,128)S(1)} %get-tuple-element.5) | data formatting | bytes 196608
